TPU v7x, 32 devices: a whole 2x2x4 slice. The times are simulated.
32 devices in a mesh: dp: 8 (over y, x, core), mp: 4 (over z).
Axes of the slice: x: 2, y: 2, z: 4, core: 2. Of those that a mesh axis runs over, the one named last changes fastest.
Arguments:
- inputs: bfloat16 [512, 65536], P('mp', 'dp'), may hold values from -24 to 24
- cotangent: bfloat16 [512, 65536], P('mp', 'dp'), may hold values from -4 to 4
- member_mask: int32 [2048, 32], P('dp'), may hold values from 0 to 1, as said below
- members: float32 [6, 32, 512], P(None, 'dp', 'mp'), may hold values from -3 to 3
- first_moment: float32 [6, 32, 512], P(None, 'dp', 'mp')
- second_moment: float32 [6, 32, 512], P(None, 'dp', 'mp'), as said below
- first_weight: float32 [512, 512], P('dp', 'mp'), may hold values from -0.25 to 0.25
- second_weight: float32 [512, 512], P('mp', 'dp'), may hold values from -0.25 to 0.25
- first_left: float32 [512, 512], P('dp', 'mp')
- first_right: float32 [512, 512], P('dp', 'mp')
- second_left: float32 [512, 512], P('mp', 'dp')
- second_right: float32 [512, 512], P('mp', 'dp')
- first_left_root: float32 [512, 512], P('dp')
- first_right_root: float32 [512, 512], P('mp')
- second_left_root: float32 [512, 512], P('mp')
- second_right_root: float32 [512, 512], P('dp')
Outputs:
- logits: bfloat16 [512, 65536], P('mp', 'dp')
- input_grad: bfloat16 [512, 65536], P('mp', 'dp')
- rms_stats: float32 [2], replicated
- first_grad: float32 [512, 512], P('dp', 'mp')
- first_new: float32 [512, 512], P('dp', 'mp')
- first_left_new: float32 [512, 512], P('dp', 'mp')
- first_right_new: float32 [512, 512], P('dp', 'mp')
- second_grad: float32 [512, 512], P('mp', 'dp')
- second_new: float32 [512, 512], P('mp', 'dp')
- second_left_new: float32 [512, 512], P('mp', 'dp')
- second_right_new: float32 [512, 512], P('mp', 'dp')
- moment_one_new: float32 [6, 32, 512], P(None, 'dp', 'mp')
- moment_two_new: float32 [6, 32, 512], P(None, 'dp', 'mp')
- members_new: float32 [6, 32, 512], P(None, 'dp', 'mp')
Inputs may be any that keep to these rules, and one draw needn't show every extreme that they name: `member_mask`: each object has between 8 and 32 trained members; some object has exactly 8 and some exactly 32. `second_moment`: positive.
All inputs are finite; a program needn't handle non-finite values.
Results may differ from a plain program's by a relative error of at most 0.0087.
Values may be sent and summed in bfloat16 or wider, within the bound.
A program may use at most 128 MiB of HBM per device.

v0:
```python
import jax
import jax.numpy as jnp
from jax import lax
from jax.sharding import PartitionSpec as P

D = 512
K = 32
STEP = 10
beta_first = 0.9
beta_second = 0.999
adam_eps = 1e-08
adam_rate = 0.2
stat_decay = 0.95
shampoo_rate = 1.0
over_rows = (((0,), (0,)), ((), ()))
over_cols = (((1,), (1,)), ((), ()))


def group_count(values):
    objects = values.shape[1] // K
    repeat = max(1, 128 // K)
    return repeat


def tiled_table(table, repeat):
    return jnp.tile(table.T, (1, repeat))


def by_member(values, table):
    width = values.shape[0]
    repeat = group_count(values)
    shaped = values.reshape(width, -1, repeat * K)
    return (shaped * tiled_table(table, repeat)[:, None, :]).reshape(values.shape)


def member_affine(values, gain, bias):
    width = values.shape[0]
    repeat = group_count(values)
    shaped = values.reshape(width, -1, repeat * K)
    return (
        shaped * tiled_table(gain, repeat)[:, None, :] + tiled_table(bias, repeat)[:, None, :]
    ).reshape(values.shape)


def member_sum(values):
    width = values.shape[0]
    repeat = group_count(values)
    partial_value = values.reshape(width, -1, repeat * K).sum(1)
    return partial_value.reshape(width, repeat, K).sum(1).T


def middle_forward(rows_in, first_low, second_low, gain_in, bias_in, row_mid):
    hidden_pre = lax.dot_general(first_low, rows_in, over_rows, preferred_element_type=jnp.float32)
    shifted = member_affine(hidden_pre, gain_in, bias_in)
    hidden, gelu_pull = jax.vjp(jax.nn.gelu, shifted)
    hidden_in = by_member(hidden, row_mid).astype(jnp.bfloat16)
    partial_value = lax.dot_general(
        second_low, hidden_in, over_rows, preferred_element_type=jnp.float32
    )
    return (hidden_pre, hidden, gelu_pull, hidden_in, partial_value)


def middle_backward(
    grad_rows,
    rows_in,
    first_low,
    second_low,
    gain_in,
    row_mid,
    hidden_pre,
    hidden,
    gelu_pull,
    hidden_in,
):
    grad_second = lax.dot_general(
        hidden_in, grad_rows, over_cols, preferred_element_type=jnp.float32
    )
    grad_hidin = jnp.dot(second_low, grad_rows, preferred_element_type=jnp.float32)
    grad_row_mid = member_sum(grad_hidin * hidden)
    grad_shift = gelu_pull(by_member(grad_hidin, row_mid))[0]
    grad_bias_in = member_sum(grad_shift)
    grad_gain_in = member_sum(grad_shift * hidden_pre)
    grad_pre = by_member(grad_shift, gain_in).astype(jnp.bfloat16)
    grad_first = lax.dot_general(rows_in, grad_pre, over_cols, preferred_element_type=jnp.float32)
    row_back = jnp.dot(first_low, grad_pre, preferred_element_type=jnp.float32)
    return (
        grad_first,
        grad_second,
        jnp.stack([grad_gain_in, grad_bias_in, grad_row_mid]),
        row_back,
    )


def on_device(
    inputs,
    cotangent,
    member_mask,
    members,
    first_moment,
    second_moment,
    first_weight,
    second_weight,
    first_left,
    first_right,
    second_left,
    second_right,
    first_left_root,
    first_right_root,
    second_left_root,
    second_right_root,
):
    high = lax.Precision.HIGHEST
    first_block, second_block, member_cols = (
        lax.all_gather(first_weight, "dp", axis=0, tiled=True),
        lax.all_gather(second_weight, "dp", axis=1, tiled=True),
        lax.all_gather(members, "dp", axis=1, tiled=True),
    )
    row_in = member_cols[0]
    gain_out = member_cols[4]
    bias_out = member_cols[5]
    values = inputs.astype(jnp.float32)
    weight_mask = member_mask.astype(jnp.float32).reshape(1, -1)
    scaled = by_member(values, row_in).astype(jnp.bfloat16)
    first_low = first_block.astype(jnp.bfloat16)
    second_low = second_block.astype(jnp.bfloat16)
    hidden_tables = member_cols[1:4]
    gathered = lax.all_gather(scaled, "mp", axis=0, tiled=True)
    hidden_pre, hidden, gelu_pull, hidden_in, partial_value = middle_forward(
        gathered, first_low, second_low, hidden_tables[0], hidden_tables[1], hidden_tables[2]
    )
    projected = lax.psum_scatter(partial_value, "mp", scatter_dimension=0, tiled=True)
    branch = member_affine(projected, gain_out, bias_out)
    logits = (values + branch).astype(jnp.bfloat16)
    first_column = (lax.axis_index("mp") == 0).astype(jnp.float32)
    totals = lax.psum(
        (
            jnp.sum(weight_mask * values * values),
            jnp.sum(weight_mask * branch * branch),
            jnp.sum(weight_mask) * first_column,
        ),
        ("dp", "mp"),
    )
    rms_stats = jnp.sqrt(jnp.stack([totals[0], totals[1]]) / (totals[2] * D))
    grad_out = cotangent.astype(jnp.float32) * weight_mask
    grad_bias_out = member_sum(grad_out)
    grad_gain_out = member_sum(grad_out * projected)
    grad_proj = by_member(grad_out, gain_out).astype(jnp.bfloat16)
    grad_full = lax.all_gather(grad_proj, "mp", axis=0, tiled=True)
    grad_first, grad_second, mid_grads, partial_back = middle_backward(
        grad_full,
        gathered,
        first_low,
        second_low,
        hidden_tables[0],
        hidden_tables[2],
        hidden_pre,
        hidden,
        gelu_pull,
        hidden_in,
    )
    grad_scaled = lax.psum_scatter(partial_back, "mp", scatter_dimension=0, tiled=True)
    grad_row_in = member_sum(grad_scaled * values)
    input_grad = (by_member(grad_scaled, row_in) + grad_out).astype(jnp.bfloat16)
    grad_vec = jnp.concatenate(
        [grad_row_in[None], mid_grads, grad_gain_out[None], grad_bias_out[None]], axis=0
    )
    first_grad, second_grad, vec_grad = (
        lax.psum_scatter(grad_first, "dp", scatter_dimension=0, tiled=True),
        lax.psum_scatter(grad_second, "dp", scatter_dimension=1, tiled=True),
        lax.psum_scatter(grad_vec, "dp", scatter_dimension=1, tiled=True),
    )
    first_rows, second_cols = (
        lax.all_gather(first_grad, "dp", axis=0, tiled=True),
        lax.all_gather(second_grad, "dp", axis=1, tiled=True),
    )
    first_total, second_total = (
        lax.all_gather(first_rows, "mp", axis=1, tiled=True),
        lax.all_gather(second_cols, "mp", axis=0, tiled=True),
    )
    owned = first_grad.shape[0]
    width = first_grad.shape[1]
    start_dp = lax.axis_index("dp") * owned
    start_mp = lax.axis_index("mp") * width
    left_rows = lax.dynamic_slice_in_dim(first_total, start_dp, owned, 0)
    right_rows = lax.dynamic_slice_in_dim(first_total, start_mp, width, 0)
    left_cols = lax.dynamic_slice_in_dim(first_total, start_dp, owned, 1)
    right_cols = lax.dynamic_slice_in_dim(first_total, start_mp, width, 1)
    first_left_new = stat_decay * first_left + (1.0 - stat_decay) * lax.dot_general(
        left_rows, right_rows, over_cols, precision=high
    )
    first_right_new = stat_decay * first_right + (1.0 - stat_decay) * lax.dot_general(
        left_cols, right_cols, over_rows, precision=high
    )
    first_step = lax.dot_general(
        jnp.dot(first_left_root, first_total, precision=high),
        first_right_root,
        over_cols,
        precision=high,
    )
    first_new = first_weight - shampoo_rate * first_step
    upper_rows = lax.dynamic_slice_in_dim(second_total, start_mp, width, 0)
    lower_rows = lax.dynamic_slice_in_dim(second_total, start_dp, owned, 0)
    upper_cols = lax.dynamic_slice_in_dim(second_total, start_mp, width, 1)
    lower_cols = lax.dynamic_slice_in_dim(second_total, start_dp, owned, 1)
    second_left_new = stat_decay * second_left + (1.0 - stat_decay) * lax.dot_general(
        upper_rows, lower_rows, over_cols, precision=high
    )
    second_right_new = stat_decay * second_right + (1.0 - stat_decay) * lax.dot_general(
        upper_cols, lower_cols, over_rows, precision=high
    )
    second_step = lax.dot_general(
        jnp.dot(second_left_root, second_total, precision=high),
        second_right_root,
        over_cols,
        precision=high,
    )
    second_new = second_weight - shampoo_rate * second_step
    moment_one = beta_first * first_moment + (1.0 - beta_first) * vec_grad
    moment_two = beta_second * second_moment + (1.0 - beta_second) * vec_grad * vec_grad
    corr_one = 1.0 - beta_first**STEP
    corr_two = 1.0 - beta_second**STEP
    members_new = members - adam_rate * (moment_one / corr_one) / (
        jnp.sqrt(moment_two / corr_two) + adam_eps
    )
    return (
        logits,
        input_grad,
        rms_stats,
        first_grad,
        first_new,
        first_left_new,
        first_right_new,
        second_grad,
        second_new,
        second_left_new,
        second_right_new,
        moment_one,
        moment_two,
        members_new,
    )


def solution(mesh):
    placed = (
        P("mp", "dp"),
        P("mp", "dp"),
        P("dp", None),
        P(None, "dp", "mp"),
        P(None, "dp", "mp"),
        P(None, "dp", "mp"),
        P("dp", "mp"),
        P("mp", "dp"),
        P("dp", "mp"),
        P("dp", "mp"),
        P("mp", "dp"),
        P("mp", "dp"),
        P("dp", None),
        P("mp", None),
        P("mp", None),
        P("dp", None),
    )
    return jax.shard_map(
        on_device,
        mesh=mesh,
        in_specs=placed,
        out_specs=(
            P("mp", "dp"),
            P("mp", "dp"),
            P(),
            P("dp", "mp"),
            P("dp", "mp"),
            P("dp", "mp"),
            P("dp", "mp"),
            P("mp", "dp"),
            P("mp", "dp"),
            P("mp", "dp"),
            P("mp", "dp"),
            P(None, "dp", "mp"),
            P(None, "dp", "mp"),
            P(None, "dp", "mp"),
        ),
        check_vma=False,
    )
```

profile of v0, /device:TPU:1, one launch (start us, length us, event | category | flops | bytes accessed | tf_op | source)
XLA Modules:
  0.0 1112.2 jit_solution(12044640973617156003)
XLA Ops:
  8.9 10.6 all_gather.27
  19.6 3.2 copy.41
  25.1 4.1 copy.39
  29.2 3.4 fusion.14
  32.7 9.2 all_gather.30
  41.9 8.2 all_gather.29
  50.1 124.2 %all-gather.7.cloned.1.call-done = bf16[512,8192]{0,1:T(8,128)(2,1)} async-done(((bf16[128,8192]{0,1:T(8,128)(2,1)}), bf16[512,8192]{0,1:T(8,128)(2,1)}) %all-gather.7.cloned.1.call-update) | async-done | bytes 8388624 | tf_op jit(solution)/shard_map/all_gather | solution.py:148
  174.3 7.8 convolution_bitcast_fusion.2
  182.1 141.2 %all-gather.5.cloned.1.call-done = bf16[512,8192]{0,1:T(8,128)(2,1)} async-done(((bf16[128,8192]{0,1:T(8,128)(2,1)}), bf16[512,8192]{0,1:T(8,128)(2,1)}) %all-gather.5.cloned.1.call-update) | async-done | bytes 8388624 | tf_op jit(solution)/shard_map/all_gather | solution.py:127
  323.3 10.1 fusion.42
  333.4 4.1 fusion.47
  341.4 6.5 fusion.45
  348.0 20.8 %reduce-scatter.12.cloned.1.call-done = f32[128,64]{0,1:T(8,128)} async-done(((f32[128,512]{0,1:T(8,128)}), f32[128,64]{0,1:T(8,128)}) %reduce-scatter.12.cloned.1.call-update) | async-done | bytes 32784 | tf_op jit(solution)/shard_map/reduce_scatter | solution.py:169
  368.8 11.2 %all_gather.34 = f32[128,512]{0,1:T(8,128)} all-gather(f32[128,64]{0,1:T(8,128)} %reduce-scatter.12.cloned.1.call-done), channel_id=1, replica_groups=mesh['dp'=8,'mp'=4] {'dp'}, dimensions={1}, use_global_device_ids=true | all-gather | bytes 294912 | tf_op jit(solution)/shard_map/all_gather | solution.py:174
  380.1 26.1 %reduce-scatter.10.cloned.1.call-done = f32[64,128]{1,0:T(8,128)} async-done(((f32[512,128]{1,0:T(8,128)}), f32[64,128]{1,0:T(8,128)}) %reduce-scatter.10.cloned.1.call-update) | async-done | bytes 32784 | tf_op jit(solution)/shard_map/reduce_scatter | solution.py:168
  406.2 11.2 %all_gather.32 = f32[512,128]{1,0:T(8,128)} all-gather(f32[64,128]{1,0:T(8,128)} %reduce-scatter.10.cloned.1.call-done), channel_id=1, replica_groups=mesh['dp'=8,'mp'=4] {'dp'}, dimensions={0}, use_global_device_ids=true | all-gather | bytes 294912 | tf_op jit(solution)/shard_map/all_gather | solution.py:173
  417.4 9.6 convolution_bitcast_fusion
  427.2 8.1 convolution_bitcast_fusion.1
  450.5 16.5 %all-gather.9.cloned.1.call-done = f32[512,512]{1,0:T(8,128)} async-done(((f32[512,128]{1,0:T(8,128)}), f32[512,512]{1,0:T(8,128)}) %all-gather.9.cloned.1.call-update) | async-done | bytes 1048592 | tf_op jit(solution)/shard_map/all_gather | solution.py:177
  477.8 271.4 %reduce-scatter.8.cloned.1.call-done = f32[128,8192]{0,1:T(8,128)} async-done(((f32[512,8192]{0,1:T(8,128)}), f32[128,8192]{0,1:T(8,128)}) %reduce-scatter.8.cloned.1.call-update) | async-done | bytes 4194320 | tf_op jit(solution)/shard_map/reduce_scatter | solution.py:161
  749.2 283.4 %reduce-scatter.6.cloned.1.call-done = f32[128,8192]{0,1:T(8,128)} async-done(((f32[512,8192]{0,1:T(8,128)}), f32[128,8192]{0,1:T(8,128)}) %reduce-scatter.6.cloned.1.call-update) | async-done | bytes 4194320 | tf_op jit(solution)/shard_map/reduce_scatter | solution.py:131
  1032.6 10.3 convert_multiply_fusion
  1051.1 40.9 %all-reduce.1 = (f32[1]{0:T(128)}, f32[1]{0:T(128)}, f32[]{:T(128)}) all-reduce(f32[1]{0:T(128)} %bitcast.29, f32[1]{0:T(128)} %bitcast.28, f32[]{:T(128)S(6)} %mul.263), channel_id=1, replica_groups=mesh['dp'=8,'mp'=4] {'dp','mp'}, use_global_device_ids=true, to_apply=%region_5.0 | all-reduce | flops 3 | bytes 24 | tf_op jit(solution)/shard_map/psum | solution.py:135
  1094.6 4.1 copy.44
  (108 shorter events, 49.9 us)
Async XLA Ops:
  7.2 464.1 %copy-start = (f32[128,512]{1,0:T(8,128)S(1)}, f32[128,512]{1,0:T(8,128)}, u32[]{:S(2)}) copy-start(f32[128,512]{1,0:T(8,128)} %param.30) | copy-start | bytes 786436
  7.2 167.1 %all-gather.7.cloned.1.call-start = ((), (), s32[]{:S(2)}) async-start(), calls=%async_computation.6 | async-start | bytes 10485760 | tf_op jit(solution)/shard_map/all_gather | solution.py:148
  22.8 6.4 copy-start.2
  25.1 298.1 %all-gather.5.cloned.1.call-start = ((), (), s32[]{:S(2)}) async-start(), calls=%async_computation.4 | async-start | bytes 10485760 | tf_op jit(solution)/shard_map/all_gather | solution.py:127
  32.6 336.2 %reduce-scatter.12.cloned.1.call-start = ((), (), s32[]{:S(2)}) async-start(), calls=%async_computation.10 | async-start | bytes 294912 | tf_op jit(solution)/shard_map/reduce_scatter | solution.py:169
  323.3 10.1 copy-start.1
  337.5 68.7 %reduce-scatter.10.cloned.1.call-start = ((), (), s32[]{:S(2)}) async-start(), calls=%async_computation.8 | async-start | bytes 294912 | tf_op jit(solution)/shard_map/reduce_scatter | solution.py:168
  348.0 98.0 %all-gather.11.cloned.1.call-start = ((), (), s32[]{:S(2)}) async-start(), calls=%async_computation.11 | async-start | bytes 1310720 | tf_op jit(solution)/shard_map/all_gather | solution.py:178
  380.0 86.9 %all-gather.9.cloned.1.call-start = ((), (), s32[]{:S(2)}) async-start(), calls=%async_computation.9 | async-start | bytes 1310720 | tf_op jit(solution)/shard_map/all_gather | solution.py:177
  417.4 331.8 %reduce-scatter.8.cloned.1.call-start = ((), (), s32[]{:S(2)}) async-start(), calls=%async_computation.7 | async-start | bytes 20971520 | tf_op jit(solution)/shard_map/reduce_scatter | solution.py:161
  427.1 605.5 %reduce-scatter.6.cloned.1.call-start = ((), (), s32[]{:S(2)}) async-start(), calls=%async_computation.5 | async-start | bytes 20971520 | tf_op jit(solution)/shard_map/reduce_scatter | solution.py:131
  435.3 669.0 %all-reduce.4.cloned.1.call-start = ((), (), s32[]{:S(2)}) async-start(), calls=%async_computation.12 | async-start | bytes 196608
  440.8 5.2 copy-start.16
  440.8 7.6 copy-start.14
  440.8 26.1 %copy-start.15 = (f32[64,128]{1,0:T(8,128)S(1)}, f32[64,128]{1,0:T(8,128)}, u32[]{:S(2)}) copy-start(f32[64,128]{1,0:T(8,128)} %param.24) | copy-start | bytes 98308
  440.8 28.1 %copy-start.17 = (f32[64,128]{1,0:T(8,128)S(1)}, f32[64,128]{1,0:T(8,128)}, u32[]{:S(2)}) copy-start(f32[64,128]{1,0:T(8,128)} %param.25) | copy-start | bytes 98308
  443.3 30.3 %copy-start.10 = (f32[64,512]{1,0:T(8,128)S(1)}, f32[64,512]{1,0:T(8,128)}, u32[]{:S(2)}) copy-start(f32[64,512]{1,0:T(8,128)} %param.31) | copy-start | bytes 393220
  443.3 31.2 %copy-start.11 = (f32[64,512]{1,0:T(8,128)S(1)}, f32[64,512]{1,0:T(8,128)}, u32[]{:S(2)}) copy-start(f32[64,512]{1,0:T(8,128)} %param.28) | copy-start | bytes 393220
  443.3 33.4 %copy-start.6 = (f32[128,512]{1,0:T(8,128)S(1)}, f32[128,512]{1,0:T(8,128)}, u32[]{:S(2)}) copy-start(f32[128,512]{1,0:T(8,128)} %param.29) | copy-start | bytes 786436
  443.3 589.3 %copy-start.3 = (bf16[128,8192]{0,1:T(8,128)(2,1)S(1)}, bf16[128,8192]{0,1:T(8,128)(2,1)}, u32[]{:S(2)}) copy-start(bf16[128,8192]{0,1:T(8,128)(2,1)} %copy-done.2) | copy-start | bytes 6291460
  1047.8 50.9 %copy-start.5 = (bf16[128,8192]{0,1:T(8,128)(2,1)S(1)}, bf16[128,8192]{0,1:T(8,128)(2,1)}, u32[]{:S(2)}) copy-start(bf16[128,8192]{0,1:T(8,128)(2,1)} %get-tuple-element.73) | copy-start | bytes 6291460
  1094.6 9.7 copy-start.13
  1094.6 9.7 copy-start.18
  1094.6 9.7 copy-start.19
  (6 other events, 11.4 us)
Sparse Core Ops, SparseCore 0:
  25.2 149.0 all-gather.6
  175.9 147.3 all-gather.4
  337.6 31.1 reduce-scatter.11
  372.6 33.5 reduce-scatter.9
  407.6 29.3 all-gather.10
  438.4 28.4 all-gather.8
  469.3 279.8 reduce-scatter.7
  751.7 280.9 reduce-scatter.5
  1051.2 52.9 all-reduce.3
where the time goes:
time: 1110 us
  waiting for transfers between devices  886 us (80%)
  blocking collectives  91.3 us (8%)
  matrix products  61.4 us (6%)
  other arithmetic  37.9 us (3%)
  local copies, waits for them, and re-layouts  18.3 us (2%)
  between operations  16.2 us (1%)
    reduce_scatter x1, waiting for transfers between devices, on_device(): lax.psum_scatter(partial_value, 'mp', scatter_dimension=0, tiled=True)  283 us
    reduce_scatter x1, waiting for transfers between devices, on_device(): lax.psum_scatter(partial_back, 'mp', scatter_dimension=0, tiled=True)  271 us
    all_gather x1, waiting for transfers between devices, on_device(): gathered = lax.all_gather(scaled, 'mp', axis=0, tiled=True)  141 us
    all_gather x1, waiting for transfers between devices, on_device(): grad_full = lax.all_gather(grad_proj, 'mp', axis=0, tiled=True)  124 us
    psum x1, blocking collectives, on_device(): lax.psum((jnp.sum(weight_mask * values * values), jnp.sum(weight_mask * b...  40.9 us
    reduce_scatter x1, waiting for transfers between devices, on_device(): lax.psum_scatter(grad_first, 'dp', scatter_dimension=0, tiled=True)  26.1 us
  transfers between devices with their start and end apart: 9, of which 8 were waited for; matrix products, arithmetic and copies ran while one was open for 7% of the time, Pallas kernels for 0%

commit v1 on v0

--- a/solution.py
+++ b/solution.py
@@ -145,7 +145,14 @@
     grad_bias_out = member_sum(grad_out)
     grad_gain_out = member_sum(grad_out * projected)
     grad_proj = by_member(grad_out, gain_out).astype(jnp.bfloat16)
-    grad_full = lax.all_gather(grad_proj, "mp", axis=0, tiled=True)
+    ways, here, hop = (lax.axis_size("mp"), lax.axis_index("mp"), grad_proj.shape[0])
+    line, have = (grad_proj, 1)
+    while have < ways:
+        line = jnp.concatenate(
+            [line, lax.ppermute(line, "mp", [(d, (d - have) % ways) for d in range(ways)])], axis=0
+        )
+        have = 2 * have
+    grad_full = jnp.roll(line, here * hop, axis=0)
     grad_first, grad_second, mid_grads, partial_back = middle_backward(
         grad_full,
         gathered,

time: 1110 us -> 1210 us (1.090)
  waiting for transfers between devices: 886 us -> 958 us
  local copies, waits for them, and re-layouts: 18.3 us -> 36 us
    ppermute x0 -> x2, waiting for transfers between devices: none -> 337 us  [on_device(): lax.ppermute(line, 'mp', [(d, (d - have) % ways) for d in range(ways)])]
    all_gather x1, waiting for transfers between devices: 141 us -> 0.01 us  [on_device(): gathered = lax.all_gather(scaled, 'mp', axis=0, tiled=True)]
    all_gather x1 -> x0, waiting for transfers between devices: 124 us -> none  [on_device(): grad_full = lax.all_gather(grad_proj, 'mp', axis=0, tiled=True)]
    unnamed x53 -> x67, local copies, waits for them, and re-layouts: 18 us -> 31.2 us
  transfers between devices with their start and end apart: 9 -> 10, of which waited for: 8 -> 8; matrix products, arithmetic and copies ran while one was open for 7% -> 7% of each run, Pallas kernels for 0% -> 0%
where the time goes in v1:
time: 1210 us; the launch traced here: 1200 us
  waiting for transfers between devices  958 us (79%)
  blocking collectives  93.3 us (8%)
  matrix products  57.2 us (5%)
  other arithmetic  38.6 us (3%)
  local copies, waits for them, and re-layouts  36 us (3%)
  between operations  16.6 us (1%)
    ppermute x2, waiting for transfers between devices, on_device(): lax.ppermute(line, 'mp', [(d, (d - have) % ways) for d in range(ways)])  337 us
    reduce_scatter x1, waiting for transfers between devices, on_device(): lax.psum_scatter(partial_value, 'mp', scatter_dimension=0, tiled=True)  284 us
    reduce_scatter x1, waiting for transfers between devices, on_device(): lax.psum_scatter(partial_back, 'mp', scatter_dimension=0, tiled=True)  271 us
    psum x1, blocking collectives, on_device(): lax.psum((jnp.sum(weight_mask * values * values), jnp.sum(weight_mask * b...  40.9 us
    unnamed x67, local copies, waits for them, and re-layouts  31.2 us
    reduce_scatter x1, waiting for transfers between devices, on_device(): lax.psum_scatter(grad_first, 'dp', scatter_dimension=0, tiled=True)  26.2 us
  transfers between devices with their start and end apart: 10, of which 8 were waited for; matrix products, arithmetic and copies ran while one was open for 7% of the time, Pallas kernels for 0%

profile of v1, /device:TPU:1, one launch (start us, length us, event | category | flops | bytes accessed | tf_op | source)
XLA Modules:
  0.0 1204.0 jit_solution(12287127302281008612)
XLA Ops:
  8.0 10.5 all_gather.24
  29.8 3.3 collective-permute-start
  33.1 109.7 %collective-permute-done = bf16[128,8192]{0,1:T(8,128)(2,1)S(1)} collective-permute-done((bf16[128,8192]{0,1:T(8,128)(2,1)S(1)}, bf16[128,8192]{0,1:T(8,128)(2,1)S(1)}, u32[]{:S(2)}, u32[]{:S(2)}) %collective-permute-start) | collective-permute-done | bytes 2097184 | tf_op jit(solution)/shard_map/ppermute | solution.py:152
  145.5 9.6 all_gather.27
  155.1 9.9 all_gather.26
  168.2 227.8 %collective-permute-done.1 = bf16[256,8192]{0,1:T(8,128)(2,1)} collective-permute-done((bf16[256,8192]{0,1:T(8,128)(2,1)}, bf16[256,8192]{0,1:T(8,128)(2,1)}, u32[]{:S(2)}, u32[]{:S(2)}) %collective-permute-start.1) | collective-permute-done | bytes 4194336 | tf_op jit(solution)/shard_map/ppermute | solution.py:152
  396.1 4.6 constant_dynamic-update-slice_fusion.3
  404.6 4.6 constant_dynamic-update-slice_fusion
  409.1 5.9 convolution_bitcast_fusion.3
  417.3 7.7 fusion.47
  425.0 4.2 fusion
  433.2 6.5 fusion.50
  439.8 20.4 %reduce-scatter.12.cloned.1.call-done = f32[128,64]{0,1:T(8,128)} async-done(((f32[128,512]{0,1:T(8,128)}), f32[128,64]{0,1:T(8,128)}) %reduce-scatter.12.cloned.1.call-update) | async-done | bytes 32784 | tf_op jit(solution)/shard_map/reduce_scatter | solution.py:176
  460.2 11.2 all_gather.30
  471.5 26.2 %reduce-scatter.10.cloned.1.call-done = f32[64,128]{1,0:T(8,128)} async-done(((f32[512,128]{1,0:T(8,128)}), f32[64,128]{1,0:T(8,128)}) %reduce-scatter.10.cloned.1.call-update) | async-done | bytes 32784 | tf_op jit(solution)/shard_map/reduce_scatter | solution.py:175
  497.7 11.2 all_gather.28
  509.0 9.7 convolution_bitcast_fusion
  518.7 8.1 convolution_bitcast_fusion.1
  541.9 16.5 %all-gather.6.cloned.1.call-done = f32[512,512]{1,0:T(8,128)} async-done(((f32[512,128]{1,0:T(8,128)}), f32[512,512]{1,0:T(8,128)}) %all-gather.6.cloned.1.call-update) | async-done | bytes 1048592 | tf_op jit(solution)/shard_map/all_gather | solution.py:184
  569.3 271.1 %reduce-scatter.8.cloned.1.call-done = f32[128,8192]{0,1:T(8,128)} async-done(((f32[512,8192]{0,1:T(8,128)}), f32[128,8192]{0,1:T(8,128)}) %reduce-scatter.8.cloned.1.call-update) | async-done | bytes 4194320 | tf_op jit(solution)/shard_map/reduce_scatter | solution.py:168
  840.5 283.5 %reduce-scatter.6.cloned.1.call-done = f32[128,8192]{0,1:T(8,128)} async-done(((f32[512,8192]{0,1:T(8,128)}), f32[128,8192]{0,1:T(8,128)}) %reduce-scatter.6.cloned.1.call-update) | async-done | bytes 4194320 | tf_op jit(solution)/shard_map/reduce_scatter | solution.py:131
  1124.0 10.4 convert_multiply_fusion
  1142.6 40.9 %all-reduce.1 = (f32[1]{0:T(128)}, f32[1]{0:T(128)}, f32[]{:T(128)}) all-reduce(f32[1]{0:T(128)} %bitcast.29, f32[1]{0:T(128)} %bitcast.28, f32[]{:T(128)S(6)} %mul.265), channel_id=1, replica_groups=mesh['dp'=8,'mp'=4] {'dp','mp'}, use_global_device_ids=true, to_apply=%region_5.0 | all-reduce | flops 3 | bytes 24 | tf_op jit(solution)/shard_map/psum | solution.py:135
  1186.0 4.1 copy.44
  (125 shorter events, 69.9 us)
Async XLA Ops:
  7.2 555.7 %copy-start = (f32[128,512]{1,0:T(8,128)S(1)}, f32[128,512]{1,0:T(8,128)}, u32[]{:S(2)}) copy-start(f32[128,512]{1,0:T(8,128)} %param.30) | copy-start | bytes 786436
  7.2 402.0 %all-gather.4.cloned.1.call-start = ((), (), s32[]{:S(2)}) async-start(), calls=%async_computation.4 | async-start | bytes 10485760 | tf_op jit(solution)/shard_map/all_gather | solution.py:127
  23.9 436.3 %reduce-scatter.12.cloned.1.call-start = ((), (), s32[]{:S(2)}) async-start(), calls=%async_computation.9 | async-start | bytes 294912 | tf_op jit(solution)/shard_map/reduce_scatter | solution.py:176
  27.4 118.0 %copy-start.2 = (bf16[128,8192]{0,1:T(8,128)(2,1)}, bf16[128,8192]{0,1:T(8,128)(2,1)S(1)}, u32[]{:S(2)}) copy-start(bf16[128,8192]{0,1:T(8,128)(2,1)S(1)} %copy.41) | copy-start | bytes 6291460
  29.8 115.6 %copy-start.5 = (bf16[128,8192]{0,1:T(8,128)(2,1)}, bf16[128,8192]{0,1:T(8,128)(2,1)S(1)}, u32[]{:S(2)}) copy-start(bf16[128,8192]{0,1:T(8,128)(2,1)S(1)} %get-tuple-element.84) | copy-start | bytes 6291460
  29.8 115.7 %copy-start.14 = (f32[64,128]{1,0:T(8,128)S(1)}, f32[64,128]{1,0:T(8,128)}, u32[]{:S(2)}) copy-start(f32[64,128]{1,0:T(8,128)} %param.22) | copy-start | bytes 98308
  29.8 115.7 %copy-start.13 = (f32[128,64]{0,1:T(8,128)S(1)}, f32[128,64]{0,1:T(8,128)}, u32[]{:S(2)}) copy-start(f32[128,64]{0,1:T(8,128)} %param.23) | copy-start | bytes 98308
  29.8 113.0 %collective-permute-start = (bf16[128,8192]{0,1:T(8,128)(2,1)S(1)}, bf16[128,8192]{0,1:T(8,128)(2,1)S(1)}, u32[]{:S(2)}, u32[]{:S(2)}) collective-permute-start(bf16[128,8192]{0,1:T(8,128)(2,1)S(1)} %get-tuple-element.84), channel_id=1, source_target_pairs={{0,3},{1,0},{2,1},{3,2},{4,7},{5,4},{6,5},{7,6},{8,11},{9,8},{10,9... | collective-permute-start | bytes 6291464 | tf_op jit(solution)/shard_map/ppermute | solution.py:152
  145.4 250.7 %collective-permute-start.1 = (bf16[256,8192]{0,1:T(8,128)(2,1)}, bf16[256,8192]{0,1:T(8,128)(2,1)}, u32[]{:S(2)}, u32[]{:S(2)}) collective-permute-start(bf16[256,8192]{0,1:T(8,128)(2,1)} %pad_maximum_fusion), channel_id=1, source_target_pairs={{0,2},{1,3},{2,0},{3,1},{4,6},{5,7},{6,4},{7,5},{8,10},{9,11},{10,... | collective-permute-start | bytes 12582920 | tf_op jit(solution)/shard_map/ppermute | solution.py:152
  168.2 232.4 %copy-start.6 = (bf16[128,8192]{0,1:T(8,128)(2,1)S(1)}, bf16[128,8192]{0,1:T(8,128)(2,1)}, u32[]{:S(2)}) copy-start(bf16[128,8192]{0,1:T(8,128)(2,1)} %copy-done.5) | copy-start | bytes 6291460
  429.2 68.5 %reduce-scatter.10.cloned.1.call-start = ((), (), s32[]{:S(2)}) async-start(), calls=%async_computation.7 | async-start | bytes 294912 | tf_op jit(solution)/shard_map/reduce_scatter | solution.py:175
  439.8 97.8 %all-gather.8.cloned.1.call-start = ((), (), s32[]{:S(2)}) async-start(), calls=%async_computation.10 | async-start | bytes 1310720 | tf_op jit(solution)/shard_map/all_gather | solution.py:185
  471.4 87.0 %all-gather.6.cloned.1.call-start = ((), (), s32[]{:S(2)}) async-start(), calls=%async_computation.8 | async-start | bytes 1310720 | tf_op jit(solution)/shard_map/all_gather | solution.py:184
  508.9 331.5 %reduce-scatter.8.cloned.1.call-start = ((), (), s32[]{:S(2)}) async-start(), calls=%async_computation.6 | async-start | bytes 20971520 | tf_op jit(solution)/shard_map/reduce_scatter | solution.py:168
  518.6 605.3 %reduce-scatter.6.cloned.1.call-start = ((), (), s32[]{:S(2)}) async-start(), calls=%async_computation.5 | async-start | bytes 20971520 | tf_op jit(solution)/shard_map/reduce_scatter | solution.py:131
  526.8 669.0 %all-reduce.4.cloned.1.call-start = ((), (), s32[]{:S(2)}) async-start(), calls=%async_computation.11 | async-start | bytes 196608
  532.3 26.1 %copy-start.20 = (f32[64,128]{1,0:T(8,128)S(1)}, f32[64,128]{1,0:T(8,128)}, u32[]{:S(2)}) copy-start(f32[64,128]{1,0:T(8,128)} %param.24) | copy-start | bytes 98308
  532.4 28.1 %copy-start.22 = (f32[64,128]{1,0:T(8,128)S(1)}, f32[64,128]{1,0:T(8,128)}, u32[]{:S(2)}) copy-start(f32[64,128]{1,0:T(8,128)} %param.25) | copy-start | bytes 98308
  534.8 30.3 %copy-start.15 = (f32[64,512]{1,0:T(8,128)S(1)}, f32[64,512]{1,0:T(8,128)}, u32[]{:S(2)}) copy-start(f32[64,512]{1,0:T(8,128)} %param.31) | copy-start | bytes 393220
  534.8 31.1 %copy-start.16 = (f32[64,512]{1,0:T(8,128)S(1)}, f32[64,512]{1,0:T(8,128)}, u32[]{:S(2)}) copy-start(f32[64,512]{1,0:T(8,128)} %param.28) | copy-start | bytes 393220
  534.8 33.5 %copy-start.11 = (f32[128,512]{1,0:T(8,128)S(1)}, f32[128,512]{1,0:T(8,128)}, u32[]{:S(2)}) copy-start(f32[128,512]{1,0:T(8,128)} %param.29) | copy-start | bytes 786436
  534.8 589.2 %copy-start.3 = (bf16[128,8192]{0,1:T(8,128)(2,1)S(1)}, bf16[128,8192]{0,1:T(8,128)(2,1)}, u32[]{:S(2)}) copy-start(bf16[128,8192]{0,1:T(8,128)(2,1)} %copy-done.2) | copy-start | bytes 6291460
  1139.3 50.9 %copy-start.10 = (bf16[128,8192]{0,1:T(8,128)(2,1)S(1)}, bf16[128,8192]{0,1:T(8,128)(2,1)}, u32[]{:S(2)}) copy-start(bf16[128,8192]{0,1:T(8,128)(2,1)} %get-tuple-element.73) | copy-start | bytes 6291460
  1186.0 9.8 copy-start.24
  (12 other events, 52.4 us)
Sparse Core Ops, SparseCore 0:
  24.0 323.5 all-gather.3
  429.3 30.8 reduce-scatter.11
  464.1 33.5 reduce-scatter.9
  499.1 29.3 all-gather.7
  529.9 28.4 all-gather.5
  560.6 279.7 reduce-scatter.7
  842.9 281.0 reduce-scatter.5
  1142.7 53.0 all-reduce.3
